TPU v7x, 32 devices: a whole 2x2x4 slice. The times are simulated.
32 devices in a mesh: rep: 4 (over y, core), fsdp: 8 (over z, x).
Axes of the slice: x: 2, y: 2, z: 4, core: 2. Of those that a mesh axis runs over, the one named last changes fastest.
Arguments:
- acts: bfloat16 [16384, 8192], P(('rep', 'fsdp')), may hold values from -12 to 12
- tok_grads: bfloat16 [16384, 1024], P(('rep', 'fsdp')), may hold values from -64 to 64
- log_ratio: float32 [16384], P(('rep', 'fsdp')), may hold values from -3 to 3
- loss_mask: int32 [16384], P(('rep', 'fsdp')), may hold values 0 or 1
- pairs: int32 [4, 8], P('rep'), may hold values from 0 to 7, each once within a row
- inner_w: float32 [4, 8192, 1024], P('rep', 'fsdp'), may hold values from -6 to 6
- adam_m: float32 [4, 8192, 1024], P('rep', 'fsdp'), may hold values from -3 to 3
- adam_v: float32 [4, 8192, 1024], P('rep', 'fsdp'), may hold values from 0.05 to 1
- anchor: float32 [8192, 1024], P('fsdp'), may hold values from -6 to 6
- outer_mom: float32 [8192, 1024], P('fsdp'), may hold values from -1.75 to 1.75
Outputs:
- input_grad: bfloat16 [16384, 8192], P(('rep', 'fsdp'))
- new_anchor: float32 [8192, 1024], P('fsdp')
- new_mom: float32 [8192, 1024], P('fsdp')
- new_m: float32 [4, 8192, 1024], P('rep', 'fsdp')
Inputs may be any that keep to these rules, and one draw needn't show every extreme that they name: Each row of pairs is a permutation of 0 to 7; chosen sequence c of a group pairs with rejected sequence 8 + pairs[r, c].
All inputs are finite; a program needn't handle non-finite values. No bound on the sum of `loss_mask` on one device may be relied on, other than what follows from the above.
Results may differ from a plain program's by a relative error of at most 0.0057.
Values may be sent and summed in bfloat16 or wider, within the bound.
A program may use at most 128 MiB of HBM per device.

v0:
```python
import jax
import jax.numpy as jnp
from jax import lax
from jax.sharding import PartitionSpec as P

D = 8192
SEQLEN = 256
SEQ_DEV = 2


dpo_beta = 0.1
decay_one = 0.9
decay_two = 0.95
inner_rate = 0.05
weight_decay = 0.1
epsilon = 1e-08
momentum = 0.9
outer_rate = 0.7


def pair_weights(seq_sums, partner):
    half_n = partner.shape[0]
    onehot = (partner[:, None] == jnp.arange(half_n, dtype=jnp.int32)[None, :]).astype(jnp.float32)
    rejected = jnp.dot(onehot, seq_sums[half_n:], precision=lax.Precision.HIGHEST)
    margin = dpo_beta * (seq_sums[:half_n] - rejected)
    pull = jax.nn.sigmoid(-margin)
    push = jnp.dot(pull, onehot, precision=lax.Precision.HIGHEST)
    return jnp.concatenate([-dpo_beta * pull, dpo_beta * push])


def outer_step(delta_avg, anchor_rows, mom_rows):
    mom_next = momentum * mom_rows + delta_avg
    anchor_next = anchor_rows - outer_rate * (delta_avg + momentum * mom_next)
    return (anchor_next, mom_next)


def local(acts, tok_grads, log_ratio, loss_mask, pairs, inner_w, adam_m, adam_v, anchor, outer_mom):
    scale = D ** (-0.5)
    mask_f = loss_mask.astype(jnp.float32)
    own_sums = (log_ratio * mask_f).reshape(SEQ_DEV, SEQLEN).sum(axis=1)
    group_sums = lax.all_gather(own_sums, "fsdp", axis=0, tiled=True)
    seq_weight = pair_weights(group_sums, pairs[0])
    mine = lax.dynamic_slice_in_dim(seq_weight, lax.axis_index("fsdp") * SEQ_DEV, SEQ_DEV)
    tok_weight = jnp.repeat(mine, SEQLEN) * mask_f
    cot = (tok_weight[:, None] * tok_grads.astype(jnp.float32)).astype(jnp.bfloat16)
    w_half = inner_w[0].astype(jnp.bfloat16)
    product = lax.dot_general(
        cot,
        lax.all_gather(w_half, "fsdp", axis=0, tiled=True),
        (((1,), (1,)), ((), ())),
        preferred_element_type=jnp.float32,
    )
    input_grad = (product * scale).astype(jnp.bfloat16)
    product = lax.dot_general(
        acts, cot, (((0,), (0,)), ((), ())), preferred_element_type=jnp.float32
    )
    grad = lax.psum_scatter(
        (product * scale).astype(jnp.bfloat16), "fsdp", scatter_dimension=0, tiled=True
    ).astype(jnp.float32)
    m_next = decay_one * adam_m[0] + (1.0 - decay_one) * grad
    v_next = decay_two * adam_v[0] + (1.0 - decay_two) * grad * grad
    inner_next = inner_w[0] - inner_rate * (
        m_next / (jnp.sqrt(v_next) + epsilon) + weight_decay * inner_w[0]
    )
    delta = anchor - inner_next
    groups = lax.axis_size("rep")
    delta_avg = lax.psum(delta, "rep") / groups
    new_anchor, new_mom = outer_step(delta_avg, anchor, outer_mom)
    return (input_grad, new_anchor, new_mom, m_next[None])


def solution(mesh):
    return jax.shard_map(
        local,
        mesh=mesh,
        in_specs=(
            P(("rep", "fsdp"), None),
            P(("rep", "fsdp"), None),
            P(("rep", "fsdp")),
            P(("rep", "fsdp")),
            P("rep", None),
            P("rep", "fsdp", None),
            P("rep", "fsdp", None),
            P("rep", "fsdp", None),
            P("fsdp", None),
            P("fsdp", None),
        ),
        out_specs=(
            P(("rep", "fsdp"), None),
            P("fsdp", None),
            P("fsdp", None),
            P("rep", "fsdp", None),
        ),
        check_vma=False,
    )
```

profile of v0, /device:TPU:13, one launch (start us, length us, event | category | flops | bytes accessed | tf_op | source)
XLA Modules:
  0.0 673.3 jit_solution(680716343340409352)
XLA Ops:
  7.2 0.0 reduce-scatter.2.cloned.1.call-start
  7.2 0.7 convert_multiply_fusion.2
  7.9 0.1 reduce_sum.9
  8.1 1.2 dynamic-slice
  10.0 0.2 dynamic-update-slice
  10.2 15.1 %all-reduce = f32[16]{0:T(128)S(1)} all-reduce(f32[16]{0:T(128)S(1)} %dynamic-update-slice), channel_id=1, replica_groups=mesh['rep'=4,'fsdp'=8] {'fsdp'}, use_global_device_ids=true, to_apply=%add | all-reduce | flops 16 | bytes 128
  25.3 0.8 broadcast_multiply_fusion
  26.1 0.9 fusion.16
  27.0 0.1 pad_maximum_fusion
  27.0 0.1 dynamic_slice.3
  27.1 0.1 broadcast_bitcast_fusion
  27.2 0.7 convert_multiply_fusion.1
  27.9 16.2 %fusion = bf16[8192,1024]{0,1:T(8,128)(2,1)} fusion(bf16[512,8192]{1,0:T(8,128)(2,1)} %param.10, bf16[512,1024]{1,0:T(8,128)(2,1)} %param.11, f32[512]{0:T(512)S(1)} %convert_multiply_fusion.1), kind=kOutput, calls=%fused_computation.1 | convolution fusion | flops 8608284672 | bytes 26216448 | tf_op jit(solution)/shard_map/dot_general | solution.py:54
  44.1 0.0 reduce-scatter.2.cloned.1.call-update
  44.1 0.0 all-gather.2.cloned.1.call-start
  44.2 5.3 copy.23
  49.5 3.8 bitcast_convert_fusion
  53.3 0.0 all-gather.2.cloned.1.call-update
  53.4 0.2 all-reduce.3.cloned.1.call-start
  53.6 5.4 copy.24
  59.0 5.4 copy.28
  64.4 5.4 copy.25
  69.8 259.3 %reduce-scatter.2.cloned.1.call-done = bf16[1024,1024]{0,1:T(8,128)(2,1)} async-done(((bf16[8192,1024]{0,1:T(8,128)(2,1)}), bf16[1024,1024]{0,1:T(8,128)(2,1)}) %reduce-scatter.2.cloned.1.call-update) | async-done | bytes 2097168 | tf_op jit(solution)/shard_map/reduce_scatter | solution.py:57
  329.0 10.2 %fusion.10 = (f32[1,1024,1024]{1,2,0:T(8,128)}, f32[1024,1024]{0,1:T(8,128)}) fusion(bf16[1024,1024]{0,1:T(8,128)(2,1)} %reduce-scatter.2.cloned.1.call-done, f32[1,1024,1024]{1,2,0:T(8,128)} %copy.24, f32[1024,1024]{0,1:T(8,128)} %copy.28, f32[1,1024,1024]{1,2,0:T(8,128)} %copy.25, f32[1,1024,1024]{1,2,0:T(8,128)} %copy.23), kind=kLoop, calls=%fused_computation.18 | loop fusion | flops 15728640 | bytes 27262976 | tf_op jit(solution)/shard_map/broadcast_in_dim | solution.py:69
  339.3 0.0 all-reduce.3.cloned.1.call-update
  339.3 0.0 copy-start
  339.3 5.9 copy.27
  345.2 212.4 %all-gather.2.cloned.1.call-done = bf16[8192,1024]{0,1:T(8,128)(2,1)} async-done(((bf16[1024,1024]{0,1:T(8,128)(2,1)}), bf16[8192,1024]{0,1:T(8,128)(2,1)}) %all-gather.2.cloned.1.call-update) | async-done | bytes 16777232 | tf_op jit(solution)/shard_map/all_gather | solution.py:49
  557.6 0.0 copy-done
  557.6 17.0 %multiply_convert_fusion.1 = bf16[512,8192]{1,0:T(8,128)(2,1)} fusion(bf16[8192,1024]{0,1:T(8,128)(2,1)} %all-gather.2.cloned.1.call-done, bf16[512,1024]{1,0:T(8,128)(2,1)S(1)} %copy-done, f32[512]{0:T(512)S(1)} %convert_multiply_fusion.1), kind=kOutput, calls=%fused_computation.2 | convolution fusion | flops 8599896064 | bytes 26216448 | tf_op jit(solution)/shard_map/dot_general | solution.py:47
  574.6 5.4 copy.31
  580.0 65.4 %all-reduce.3.cloned.1.call-done = f32[1024,1024]{0,1:T(8,128)} async-done(((f32[1024,1024]{0,1:T(8,128)}), f32[1024,1024]{0,1:T(8,128)}) %all-reduce.3.cloned.1.call-update) | async-done | bytes 4194320 | tf_op jit(solution)/shard_map/psum | solution.py:67
  645.4 10.6 %multiply_add_fusion = (f32[1024,1024]{0,1:T(8,128)}, f32[1024,1024]{0,1:T(8,128)}) fusion(f32[1024,1024]{0,1:T(8,128)} %copy.27, f32[1024,1024]{0,1:T(8,128)} %all-reduce.3.cloned.1.call-done, f32[1024,1024]{0,1:T(8,128)} %copy.28), kind=kLoop, calls=%fused_computation.17 | loop fusion | flops 7340032 | bytes 20971520 | tf_op jit(solution)/shard_map/add | solution.py:32
  656.1 5.3 copy.29
  661.4 5.3 copy.30
  (3 shorter events, 0.0 us)
Async XLA Ops:
  7.2 321.9 %reduce-scatter.2.cloned.1.call-start = ((), (), s32[]{:S(2)}) async-start(), calls=%async_computation.2 | async-start | bytes 18874368 | tf_op jit(solution)/shard_map/reduce_scatter | solution.py:57
  44.1 513.5 %all-gather.2.cloned.1.call-start = ((), (), s32[]{:S(2)}) async-start(), calls=%async_computation.1 | async-start | bytes 18874368 | tf_op jit(solution)/shard_map/all_gather | solution.py:49
  53.4 592.1 %all-reduce.3.cloned.1.call-start = ((), (), s32[]{:S(2)}) async-start(), calls=%async_computation.3 | async-start | bytes 8388608 | tf_op jit(solution)/shard_map/psum | solution.py:67
  339.3 218.3 %copy-start = (bf16[512,1024]{1,0:T(8,128)(2,1)S(1)}, bf16[512,1024]{1,0:T(8,128)(2,1)}, u32[]{:S(2)}) copy-start(bf16[512,1024]{1,0:T(8,128)(2,1)} %param.11) | copy-start | bytes 3145732
Sparse Core Ops, SparseCore 0:
  44.2 284.7 reduce-scatter.1
  331.5 226.1 all-gather.1
  560.1 85.2 all-reduce.2
where the time goes:
time: 676 us; the launch traced here: 673 us
  waiting for transfers between devices  537 us (79%)
  local copies, waits for them, and re-layouts  45.2 us (7%)
  matrix products  34.9 us (5%)
  other arithmetic  26.3 us (4%)
  blocking collectives  15.1 us (2%)
  between operations  14.4 us (2%)
    reduce_scatter x1, waiting for transfers between devices, local(): lax.psum_scatter((product * scale).astype(jnp.bfloat16), 'fsdp', scatter_...  259 us
    all_gather x1, waiting for transfers between devices, local(): lax.all_gather(w_half, 'fsdp', axis=0, tiled=True)  212 us
    psum x1, waiting for transfers between devices, local(): delta_avg = lax.psum(delta, 'rep') / groups  65.4 us
    unnamed x15, local copies, waits for them, and re-layouts  45.1 us
    dot_general x1, matrix products, local(): lax.dot_general(cot, lax.all_gather(w_half, 'fsdp', axis=0, tiled=True),...  17 us
    dot_general x1, matrix products, local(): lax.dot_general(acts, cot, (((0,), (0,)), ((), ())), preferred_element_ty...  16.2 us
    unnamed x1, blocking collectives  15.1 us
  transfers between devices with their start and end apart: 3, of which 3 were waited for; matrix products, arithmetic and copies ran while one was open for 9% of the time, Pallas kernels for 0%

commit v1 on v0

v1 whole, which is shorter than its diff:
```python
import functools

import jax
import jax.numpy as jnp
from jax import lax
from jax.experimental import pallas as pl
from jax.experimental.pallas import tpu as pltpu
from jax.sharding import PartitionSpec as P

SEQLEN = 256

dpo_beta = 0.1
decay_one = 0.9
decay_two = 0.95
inner_rate = 0.05
weight_decay = 0.1
epsilon = 1e-08
momentum = 0.9
outer_rate = 0.7

MESH = pl.DeviceIdType.MESH


def pair_signs(partner, half_n):
    cols = jnp.arange(2 * half_n, dtype=jnp.int32)[None, :]
    chosen = jnp.arange(half_n, dtype=jnp.int32)[:, None]
    of_pair = (cols == chosen).astype(jnp.float32) - (cols == half_n + partner[:, None]).astype(jnp.float32)
    onehot = (partner[:, None] == jnp.arange(half_n, dtype=jnp.int32)[None, :]).astype(jnp.float32)
    of_rejected = jnp.sum(onehot[:, :, None] * of_pair[:, None, :], axis=0)
    return jnp.concatenate([of_pair, of_rejected])


def exchange_kernel(
    size, scale, acts, grads, w_own, sums, signs, input_grad, grad,
    all_sums, act, cot, w_all, up, down, stage,
    sums_tx, sums_rx, g_sem, local_sem, act_local, act_tx, act_rx, z_tx, z_rx, ig_local, ig_tx, ig_rx,
):
    n = size // 2
    me = lax.axis_index("fsdp")
    z, x = lax.div(me, 2), lax.rem(me, 2)
    peer = z * 2 + (1 - x)
    above, below = lax.rem(me + 2, size), lax.rem(me + size - 2, size)
    rows = acts.shape[0]
    feats, width = w_own.shape
    part = min(256, feats)
    parts = feats // part
    seqs = rows // SEQLEN

    def remote(src, dst, tx, rx, target):
        return pltpu.make_async_remote_copy(
            src_ref=src, dst_ref=dst, send_sem=tx, recv_sem=rx,
            device_id={"fsdp": target}, device_id_type=MESH,
        )

    def columns(block):
        return pl.ds(pl.multiple_of(block * feats, feats), feats)

    def load_acts(j):
        return pltpu.make_async_copy(
            acts.at[:, columns(j * 2 + x)], act.at[j, pl.ds(0, rows)], act_local.at[j])

    def send_block(j):
        return remote(
            acts.at[:, columns(j * 2 + 1 - x)], act.at[j, pl.ds(rows, rows)], act_tx.at[j], act_rx.at[j], peer)

    def send_acts(d):
        @pl.when(z + d <= n - 1)
        def _():
            send_block(z + d).start()

        @pl.when(jnp.logical_and(d > 0, z - d >= 0))
        def _():
            send_block(z - d).start()

    def w_copy(way, j, t_send, t_recv, target):
        return remote(w_all.at[j], w_all.at[j], z_tx.at[way, t_send], z_rx.at[way, t_recv], target)

    def sum_copy(way, j, t_send, t_recv, target):
        buf = up if way == 0 else down
        return remote(buf.at[j], buf.at[j], z_tx.at[way, t_send], z_rx.at[way, t_recv], target)

    own_w = pltpu.make_async_copy(w_own, w_all.at[z], local_sem.at[0])
    own_g = pltpu.make_async_copy(grads, cot.at[pl.ds(0, rows)], local_sem.at[1])
    own_w.start()
    own_g.start()

    @pl.loop(0, n)
    def _(j):
        load_acts(j).start()

    all_sums[me] = sums[...]

    barrier = pltpu.get_barrier_semaphore()

    @pl.loop(1, size)
    def _(k):
        pl.semaphore_signal(
            barrier, inc=1, device_id={"fsdp": lax.rem(me + k, size)}, device_id_type=MESH)

    pl.semaphore_wait(barrier, size - 1)

    @pl.loop(1, size)
    def _(k):
        remote(sums, all_sums.at[me], sums_tx.at[k], sums_rx.at[me], lax.rem(me + k, size)).start()

    peer_g = remote(grads, cot.at[pl.ds(rows, rows)], g_sem.at[0], g_sem.at[1], peer)
    peer_g.start()
    own_w.wait()

    @pl.when(z < n - 1)
    def _():
        w_copy(0, z, 0, 0, above).start()

    @pl.when(z > 0)
    def _():
        w_copy(1, z, 0, 0, below).start()

    send_acts(n - 1)

    @pl.loop(1, size)
    def _(k):
        source = lax.rem(me + k, size)
        remote(sums, all_sums.at[source], sums_tx.at[k], sums_rx.at[source], peer).wait_recv()

    own_g.wait()
    peer_g.wait_recv()
    if n >= 2:
        send_acts(n - 2)
    half_n = size * seqs // 2
    for q in range(2 * seqs):
        owner = me if q < seqs else peer
        seq = owner * seqs + q % seqs
        margin = dpo_beta * jnp.sum(jnp.sum(all_sums[...] * signs[q], axis=0), axis=0, keepdims=True)
        pull = 1.0 / (1.0 + jnp.exp(margin))
        weight = jnp.where(seq < half_n, -dpo_beta, dpo_beta) * pull
        span = pl.ds(q * SEQLEN, SEQLEN)
        for lane in range(0, width, 128):
            cell = cot[span, lane:lane + 128].astype(jnp.float32)
            cot[span, lane:lane + 128] = (weight * cell).astype(jnp.bfloat16)

    def partial(j):
        load_acts(j).wait()
        send_block(j).wait_recv()

        @pl.loop(0, parts)
        def _(c):
            span = pl.ds(pl.multiple_of(c * part, part), part)
            grad[span, :] = scale * lax.dot_general(
                act[j, :, span], cot[...], (((0,), (0,)), ((), ())), preferred_element_type=jnp.float32)

    def add_in(buf, j):
        @pl.loop(0, parts)
        def _(c):
            span = pl.ds(pl.multiple_of(c * part, part), part)
            grad[span, :] = grad[span, :] + buf[j, span, :].astype(jnp.float32)

    def pass_on(way, j, t):
        buf = up if way == 0 else down
        has_source = z > 0 if way == 0 else z < n - 1
        partial(j)

        @pl.when(has_source)
        def _():
            sum_copy(way, j, t, t - 1, peer).wait_recv()

            @pl.loop(0, parts)
            def _(c):
                span = pl.ds(pl.multiple_of(c * part, part), part)
                buf[j, span, :] = (grad[span, :] + buf[j, span, :].astype(jnp.float32)).astype(jnp.bfloat16)

        @pl.when(jnp.logical_not(has_source))
        def _():
            @pl.loop(0, parts)
            def _(c):
                span = pl.ds(pl.multiple_of(c * part, part), part)
                buf[j, span, :] = grad[span, :].astype(jnp.bfloat16)

        sum_copy(way, j, t, t, above if way == 0 else below).start()

    def ig_keep(j):
        return pltpu.make_async_copy(
            stage.at[j, pl.ds(0, rows)], input_grad.at[:, columns(j * 2 + x)], ig_local.at[j])

    def ig_send(j):
        return remote(
            stage.at[j, pl.ds(rows, rows)], input_grad.at[:, columns(j * 2 + x)], ig_tx.at[j], ig_rx.at[j], peer)

    def ig_arrival(j):
        return remote(
            stage.at[j, pl.ds(rows, rows)], input_grad.at[:, columns(j * 2 + 1 - x)], ig_tx.at[j], ig_rx.at[j], peer)

    def ig_block(j):
        @pl.loop(0, parts)
        def _(c):
            span = pl.ds(pl.multiple_of(c * part, part), part)
            stage[j, :, span] = (scale * lax.dot_general(
                cot[...], w_all[j, span, :], (((1,), (1,)), ((), ())), preferred_element_type=jnp.float32
            )).astype(jnp.bfloat16)

        ig_keep(j).start()
        ig_send(j).start()

    def slot(t, carry):
        d = n - t

        @pl.when(z >= t)
        def _():
            w_copy(0, z - t, t, t - 1, peer).wait_recv()

            @pl.when(z < n - 1)
            def _():
                w_copy(0, z - t, t, t, above).start()

        @pl.when(z + t <= n - 1)
        def _():
            w_copy(1, z + t, t, t - 1, peer).wait_recv()

            @pl.when(z > 0)
            def _():
                w_copy(1, z + t, t, t, below).start()

        @pl.when(z + d <= n - 1)
        def _():
            pass_on(0, z + d, t)

        @pl.when(z - d >= 0)
        def _():
            pass_on(1, z - d, t)

        @pl.when(d >= 2)
        def _():
            send_acts(d - 2)

        @pl.when(t == 1)
        def _():
            ig_block(z)

        @pl.when(z >= t)
        def _():
            ig_block(z - t)

        @pl.when(z + t <= n - 1)
        def _():
            ig_block(z + t)

        return carry

    lax.fori_loop(1, n, slot, 0)

    partial(z)

    @pl.when(z > 0)
    def _():
        sum_copy(0, z, n - 1, n - 1, peer).wait_recv()
        add_in(up, z)

    @pl.when(z < n - 1)
    def _():
        sum_copy(1, z, n - 1, n - 1, peer).wait_recv()
        add_in(down, z)

    @pl.loop(1, size)
    def _(k):
        remote(sums, all_sums.at[me], sums_tx.at[k], sums_rx.at[me], peer).wait_send()

    peer_g.wait_send()

    @pl.loop(0, n)
    def _(j):
        send_block(j).wait_send()
        w_way = j

        @pl.when(z < n - 1)
        def _():
            sum_copy(0, w_way, j, j, peer).wait_send()

        @pl.when(z > 0)
        def _():
            sum_copy(1, w_way, j, j, peer).wait_send()

        ig_keep(j).wait()
        ig_send(j).wait_send()
        ig_arrival(j).wait_recv()


def exchange(size, scale, acts, grads, w_half, sums, signs):
    n = size // 2
    rows, model = acts.shape
    feats, width = w_half.shape
    dma = pltpu.SemaphoreType.DMA
    bf16 = jnp.bfloat16
    anywhere = pl.BlockSpec(memory_space=pl.ANY)
    vmem = pl.BlockSpec(memory_space=pltpu.VMEM)
    return pl.pallas_call(
        functools.partial(exchange_kernel, size, scale),
        out_shape=(
            jax.ShapeDtypeStruct((rows, model), bf16),
            jax.ShapeDtypeStruct((feats, width), jnp.float32),
        ),
        in_specs=[anywhere, anywhere, anywhere, vmem, vmem],
        out_specs=(anywhere, vmem),
        scratch_shapes=[
            pltpu.VMEM((size,) + sums.shape, jnp.float32),
            pltpu.VMEM((n, 2 * rows, feats), bf16),
            pltpu.VMEM((2 * rows, width), bf16),
            pltpu.VMEM((n, feats, width), bf16),
            pltpu.VMEM((n, feats, width), bf16),
            pltpu.VMEM((n, feats, width), bf16),
            pltpu.VMEM((n, 2 * rows, feats), bf16),
            dma((size,)), dma((size,)), dma((2,)), dma((2,)),
            dma((n,)), dma((n,)), dma((n,)),
            dma((2, n)), dma((2, n)),
            dma((n,)), dma((n,)), dma((n,)),
        ],
        compiler_params=pltpu.CompilerParams(
            collective_id=0, has_side_effects=True, vmem_limit_bytes=60 * 1024 * 1024),
        cost_estimate=pl.CostEstimate(
            flops=8 * rows * model * width, bytes_accessed=6 * rows * model, transcendentals=0),
    )(acts, grads, w_half, sums, signs)


def outer_step(delta_avg, anchor_rows, mom_rows):
    mom_next = momentum * mom_rows + delta_avg
    anchor_next = anchor_rows - outer_rate * (delta_avg + momentum * mom_next)
    return (anchor_next, mom_next)


def local(acts, tok_grads, log_ratio, loss_mask, pairs, inner_w, adam_m, adam_v, anchor, outer_mom):
    size = lax.axis_size("fsdp")
    rows, model = acts.shape
    seqs = rows // SEQLEN
    scale = model ** (-0.5)
    mask_f = loss_mask.astype(jnp.float32)
    own_sums = (log_ratio * mask_f).reshape(seqs, SEQLEN).sum(axis=1)
    tile = -(-seqs // 8) * 8
    sums = jnp.zeros((tile, 128), jnp.float32).at[:seqs].set(jnp.broadcast_to(own_sums[:, None], (seqs, 128)))
    me = lax.axis_index("fsdp")
    peer = me + 1 - 2 * lax.rem(me, 2)
    table = pair_signs(pairs[0], size * seqs // 2)
    ours = jnp.concatenate([
        lax.dynamic_slice_in_dim(table, me * seqs, seqs),
        lax.dynamic_slice_in_dim(table, peer * seqs, seqs),
    ]).reshape(2 * seqs, size, seqs)
    signs = jnp.broadcast_to(
        jnp.pad(ours, ((0, 0), (0, 0), (0, tile - seqs)))[..., None], (2 * seqs, size, tile, 128))
    grads = jnp.where(loss_mask[:, None] != 0, tok_grads, jnp.zeros_like(tok_grads))
    w_half = inner_w[0].astype(jnp.bfloat16)
    input_grad, grad = exchange(size, scale, acts, grads, w_half, sums, signs)
    m_next = decay_one * adam_m[0] + (1.0 - decay_one) * grad
    v_next = decay_two * adam_v[0] + (1.0 - decay_two) * grad * grad
    inner_next = inner_w[0] - inner_rate * (
        m_next / (jnp.sqrt(v_next) + epsilon) + weight_decay * inner_w[0]
    )
    delta = anchor - inner_next
    groups = lax.axis_size("rep")
    delta_avg = lax.psum(delta, "rep") / groups
    new_anchor, new_mom = outer_step(delta_avg, anchor, outer_mom)
    return (input_grad, new_anchor, new_mom, m_next[None])


def solution(mesh):
    return jax.shard_map(
        local,
        mesh=mesh,
        in_specs=(
            P(("rep", "fsdp"), None),
            P(("rep", "fsdp"), None),
            P(("rep", "fsdp")),
            P(("rep", "fsdp")),
            P("rep", None),
            P("rep", "fsdp", None),
            P("rep", "fsdp", None),
            P("rep", "fsdp", None),
            P("fsdp", None),
            P("fsdp", None),
        ),
        out_specs=(
            P(("rep", "fsdp"), None),
            P("fsdp", None),
            P("fsdp", None),
            P("rep", "fsdp", None),
        ),
        check_vma=False,
    )
```

time: 676 us -> 353 us (0.52)
  waiting for transfers between devices: 537 us -> 85.7 us
  Pallas kernels: 0 us -> 211 us
  local copies, waits for them, and re-layouts: 45.2 us -> 9.44 us
  matrix products: 34.9 us -> 0 us
  blocking collectives: 15.1 us -> 0 us
    reduce_scatter x1 -> x0, waiting for transfers between devices: 259 us -> none  [local(): lax.psum_scatter((product * scale).astype(jnp.bfloat16), 'fsdp', scatter_...]
    all_gather x1 -> x0, waiting for transfers between devices: 212 us -> none  [local(): lax.all_gather(w_half, 'fsdp', axis=0, tiled=True)]
    pallas_call x0 -> x1, Pallas kernels: none -> 211 us  [exchange(): pl.pallas_call(functools.partial(exchange_kernel, size, scale), out_shape...]
    unnamed x15 -> x4, local copies, waits for them, and re-layouts: 45.1 us -> 7.91 us
    dot_general x4 -> x0, matrix products: 34.9 us -> none  [the longest x1 17 us: local(): lax.dot_general(cot, lax.all_gather(w_half, 'fsdp', axis=0, tiled=True),...]
    psum x1, waiting for transfers between devices: 65.4 us -> 85.7 us  [local(): delta_avg = lax.psum(delta, 'rep') / groups]
    unnamed x1 -> x0, blocking collectives: 15.1 us -> none
    sub x0 -> x2, other arithmetic: none -> 10.7 us  [the longest x1 10.6 us: outer_step(): anchor_next = anchor_rows - outer_rate * (delta_avg + momentum * mom_next)]
  transfers between devices with their start and end apart: 3 -> 1, of which waited for: 3 -> 1; matrix products, arithmetic and copies ran while one was open for 9% -> 0% of each run, Pallas kernels for 0% -> 0%
where the time goes in v1:
time: 353 us; the launch traced here: 350 us
  Pallas kernels  211 us (60%)
  waiting for transfers between devices  85.7 us (24%)
  other arithmetic  30 us (8%)
  between operations  14.1 us (4%)
  local copies, waits for them, and re-layouts  9.44 us (3%)
    pallas_call x1, Pallas kernels, exchange(): pl.pallas_call(functools.partial(exchange_kernel, size, scale), out_shape...  211 us
    psum x1, waiting for transfers between devices, local(): delta_avg = lax.psum(delta, 'rep') / groups  85.7 us
    broadcast_in_dim x1, other arithmetic, local(): return (input_grad, new_anchor, new_mom, m_next[None])  11.3 us
    sub x1, other arithmetic, outer_step(): anchor_next = anchor_rows - outer_rate * (delta_avg + momentum * mom_next)  10.6 us
    unnamed x4, local copies, waits for them, and re-layouts  7.91 us
  transfers between devices with their start and end apart: 1, of which 1 were waited for; matrix products, arithmetic and copies ran while one was open for 0% of the time, Pallas kernels for 0%

profile of v1, /device:TPU:13, one launch (start us, length us, event | category | flops | bytes accessed | tf_op | source)
XLA Modules:
  0.0 350.2 jit_solution(11814654156204596206)
XLA Ops:
  7.2 0.0 copy-start
  7.2 0.0 all-reduce.4.cloned.1.call-start
  7.2 0.8 broadcast_compare_fusion
  8.0 0.7 broadcast_add_fusion
  8.7 0.7 convert_multiply_fusion
  9.4 0.1 reduce_sum.18
  9.5 0.1 convert_subtract_fusion
  9.6 0.7 fusion.9
  10.3 0.1 multiply_reduce_fusion
  10.4 0.1 copy.18
  10.5 0.1 copy.20
  10.6 3.8 %bitcast_convert_fusion.w_own = bf16[1024,1024]{1,0:T(8,128)(2,1)} fusion(f32[1,1024,1024]{2,1,0:T(8,128)} %param.17), kind=kLoop, calls=%fused_computation.11 | loop fusion | flops 1048576 | bytes 6291456 | tf_op jit(solution)/shard_map/convert_element_type | solution.py:347
  14.5 0.0 copy-done
  14.5 1.1 broadcast_select_fusion.grads
  15.6 0.7 scatter.8.sums
  16.3 0.8 broadcast_in_dim.13.signs
  17.0 210.9 %shard_map.129 = (bf16[512,8192]{1,0:T(8,128)(2,1)}, f32[1024,1024]{1,0:T(8,128)}) custom-call(bf16[512,8192]{1,0:T(8,128)(2,1)} %acts.1, bf16[512,1024]{1,0:T(8,128)(2,1)} %broadcast_select_fusion.grads, bf16[1024,1024]{1,0:T(8,128)(2,1)} %bitcast_convert_fusion.w_own, f32[8,128]{1,0:T(8,128)} %scatter.8.sums, f32[4,8,8,128]{3,2,1,0:T(8,128)} %broadcast_in_dim.13.signs), custom_call_target="tpu_custom_call" | custom-call | flops 34359738368 | bytes 25165824 | tf_op jit(solution)/shard_map/pallas_call | solution.py:294
  227.9 11.3 %fusion.8 = (f32[1,1024,1024]{2,1,0:T(8,128)}, f32[1024,1024]{1,0:T(8,128)}) fusion(f32[1024,1024]{1,0:T(8,128)} %get-tuple-element.19, f32[1,1024,1024]{2,1,0:T(8,128)} %param.18, f32[1024,1024]{1,0:T(8,128)} %param.20, f32[1,1024,1024]{2,1,0:T(8,128)} %param.19, f32[1,1024,1024]{2,1,0:T(8,128)} %param.17), kind=kLoop, calls=%fused_computation.14 | loop fusion | flops 14680064 | bytes 29360128 | tf_op jit(solution)/shard_map/broadcast_in_dim | solution.py:358
  239.2 0.0 all-reduce.4.cloned.1.call-update
  239.3 85.7 %all-reduce.4.cloned.1.call-done = f32[1024,1024]{1,0:T(8,128)} async-done(((f32[1024,1024]{1,0:T(8,128)}), f32[1024,1024]{1,0:T(8,128)}) %all-reduce.4.cloned.1.call-update) | async-done | bytes 4194320 | tf_op jit(solution)/shard_map/psum | solution.py:356
  324.9 10.6 %multiply_subtract_fusion = (f32[1024,1024]{1,0:T(8,128)}, f32[1024,1024]{1,0:T(8,128)}) fusion(f32[1024,1024]{1,0:T(8,128)} %param.20, f32[1024,1024]{1,0:T(8,128)} %all-reduce.4.cloned.1.call-done, f32[1024,1024]{1,0:T(8,128)} %param.21), kind=kLoop, calls=%fused_computation.12 | loop fusion | flops 7340032 | bytes 20971520 | tf_op jit(solution)/shard_map/sub | solution.py:324
  335.6 7.8 %copy.23 = bf16[512,8192]{1,0:T(8,128)(2,1)} copy(bf16[512,8192]{1,0:T(8,128)(2,1)} %get-tuple-element.30) | data formatting | bytes 16777216
  (5 shorter events, 0.1 us)
Async XLA Ops:
  7.2 7.3 %copy-start = (bf16[512,1024]{1,0:T(8,128)(2,1)S(1)}, bf16[512,1024]{1,0:T(8,128)(2,1)}, u32[]{:S(2)}) copy-start(bf16[512,1024]{1,0:T(8,128)(2,1)} %param.13) | copy-start | bytes 3145732
  7.2 317.8 %all-reduce.4.cloned.1.call-start = ((), (), s32[]{:S(2)}) async-start(), calls=%async_computation | async-start | bytes 8388608 | tf_op jit(solution)/shard_map/psum | solution.py:356
Sparse Core Ops, SparseCore 0:
  239.4 85.5 all-reduce.3

commit v2 on v1

--- a/solution.py
+++ b/solution.py
@@ -18,6 +18,8 @@
 momentum = 0.9
 outer_rate = 0.7
 
+CHUNKS = 8
+
 MESH = pl.DeviceIdType.MESH
 
 
@@ -31,9 +33,11 @@
 
 
 def exchange_kernel(
-    size, scale, acts, grads, w_own, sums, signs, input_grad, grad,
-    all_sums, act, cot, w_all, up, down, stage,
+    size, groups, scale, acts, grads, w_own, sums, signs, inner_w, adam_m, adam_v, anchor,
+    input_grad, grad, delta_sum,
+    all_sums, act, cot, w_all, running, stage, state, delta, core_in, y_parts,
     sums_tx, sums_rx, g_sem, local_sem, act_local, act_tx, act_rx, z_tx, z_rx, ig_local, ig_tx, ig_rx,
+    state_sem, core_tx, core_rx, y_tx, y_rx, back_tx, back_rx,
 ):
     n = size // 2
     me = lax.axis_index("fsdp")
@@ -45,12 +49,30 @@
     part = min(256, feats)
     parts = feats // part
     seqs = rows // SEQLEN
-
-    def remote(src, dst, tx, rx, target):
+    chunk = feats // CHUNKS
+    half = chunk // 2
+    pairs_y = groups // 2
+    group = lax.axis_index("rep")
+    y, core = lax.div(group, 2), lax.rem(group, 2)
+    core_peer = y * 2 + (1 - core)
+
+    def remote(src, dst, tx, rx, target, axis="fsdp"):
         return pltpu.make_async_remote_copy(
             src_ref=src, dst_ref=dst, send_sem=tx, recv_sem=rx,
-            device_id={"fsdp": target}, device_id_type=MESH,
+            device_id={axis: target}, device_id_type=MESH,
         )
+
+    def y_peer(k):
+        return lax.rem(y + k, pairs_y) * 2 + core
+
+    def chunk_rows(c):
+        return pl.ds(pl.multiple_of(c * chunk, chunk), chunk)
+
+    def half_rows(c, which):
+        return pl.ds(pl.multiple_of(c * chunk + which * half, half), half)
+
+    def packed_rows(c):
+        return pl.ds(pl.multiple_of(c * half, half), half)
 
     def columns(block):
         return pl.ds(pl.multiple_of(block * feats, feats), feats)
@@ -72,17 +94,38 @@
         def _():
             send_block(z - d).start()
 
-    def w_copy(way, j, t_send, t_recv, target):
-        return remote(w_all.at[j], w_all.at[j], z_tx.at[way, t_send], z_rx.at[way, t_recv], target)
-
-    def sum_copy(way, j, t_send, t_recv, target):
-        buf = up if way == 0 else down
-        return remote(buf.at[j], buf.at[j], z_tx.at[way, t_send], z_rx.at[way, t_recv], target)
+    def z_copy(buf, slot_at, way, t_send, t_recv, c, target):
+        at = buf.at[slot_at, chunk_rows(c)]
+        return remote(at, at, z_tx.at[way, t_send, c], z_rx.at[way, t_recv, c], target)
+
+    def w_send(way, j, t, target):
+        @pl.loop(0, CHUNKS)
+        def _(c):
+            z_copy(w_all, j, way, t, t, c, target).start()
+
+    def w_relay(way, j, t, target, further):
+        @pl.loop(0, CHUNKS)
+        def _(c):
+            z_copy(w_all, j, way, t, t - 1, c, peer).wait_recv()
+
+            @pl.when(further)
+            def _():
+                z_copy(w_all, j, way, t, t, c, target).start()
+
+    def load_state(c):
+        at = lax.rem(c, 2)
+        return [
+            pltpu.make_async_copy(array.at[chunk_rows(c)], state.at[at, i], state_sem.at[at, i])
+            for i, array in enumerate((inner_w, adam_m, adam_v, anchor))
+        ]
 
     own_w = pltpu.make_async_copy(w_own, w_all.at[z], local_sem.at[0])
     own_g = pltpu.make_async_copy(grads, cot.at[pl.ds(0, rows)], local_sem.at[1])
     own_w.start()
     own_g.start()
+    for c in range(2):
+        for copy in load_state(c):
+            copy.start()
 
     @pl.loop(0, n)
     def _(j):
@@ -97,7 +140,10 @@
         pl.semaphore_signal(
             barrier, inc=1, device_id={"fsdp": lax.rem(me + k, size)}, device_id_type=MESH)
 
-    pl.semaphore_wait(barrier, size - 1)
+    pl.semaphore_signal(barrier, inc=1, device_id={"rep": core_peer}, device_id_type=MESH)
+    for k in range(1, pairs_y):
+        pl.semaphore_signal(barrier, inc=1, device_id={"rep": y_peer(k)}, device_id_type=MESH)
+    pl.semaphore_wait(barrier, size - 1 + pairs_y)
 
     @pl.loop(1, size)
     def _(k):
@@ -109,11 +155,11 @@
 
     @pl.when(z < n - 1)
     def _():
-        w_copy(0, z, 0, 0, above).start()
+        w_send(0, z, 0, above)
 
     @pl.when(z > 0)
     def _():
-        w_copy(1, z, 0, 0, below).start()
+        w_send(1, z, 0, below)
 
     send_acts(n - 1)
 
@@ -148,34 +194,27 @@
             grad[span, :] = scale * lax.dot_general(
                 act[j, :, span], cot[...], (((0,), (0,)), ((), ())), preferred_element_type=jnp.float32)
 
-    def add_in(buf, j):
-        @pl.loop(0, parts)
-        def _(c):
-            span = pl.ds(pl.multiple_of(c * part, part), part)
-            grad[span, :] = grad[span, :] + buf[j, span, :].astype(jnp.float32)
-
     def pass_on(way, j, t):
-        buf = up if way == 0 else down
+        at = j + 1 if way == 0 else j
         has_source = z > 0 if way == 0 else z < n - 1
+        target = above if way == 0 else below
         partial(j)
 
-        @pl.when(has_source)
-        def _():
-            sum_copy(way, j, t, t - 1, peer).wait_recv()
-
-            @pl.loop(0, parts)
-            def _(c):
-                span = pl.ds(pl.multiple_of(c * part, part), part)
-                buf[j, span, :] = (grad[span, :] + buf[j, span, :].astype(jnp.float32)).astype(jnp.bfloat16)
-
-        @pl.when(jnp.logical_not(has_source))
-        def _():
-            @pl.loop(0, parts)
-            def _(c):
-                span = pl.ds(pl.multiple_of(c * part, part), part)
-                buf[j, span, :] = grad[span, :].astype(jnp.bfloat16)
-
-        sum_copy(way, j, t, t, above if way == 0 else below).start()
+        @pl.loop(0, CHUNKS)
+        def _(c):
+            span = chunk_rows(c)
+
+            @pl.when(has_source)
+            def _():
+                z_copy(running, at, way, t, t - 1, c, peer).wait_recv()
+                running[at, span, :] = (
+                    grad[span, :] + running[at, span, :].astype(jnp.float32)).astype(jnp.bfloat16)
+
+            @pl.when(jnp.logical_not(has_source))
+            def _():
+                running[at, span, :] = grad[span, :].astype(jnp.bfloat16)
+
+            z_copy(running, at, way, t, t, c, target).start()
 
     def ig_keep(j):
         return pltpu.make_async_copy(
@@ -205,19 +244,11 @@
 
         @pl.when(z >= t)
         def _():
-            w_copy(0, z - t, t, t - 1, peer).wait_recv()
-
-            @pl.when(z < n - 1)
-            def _():
-                w_copy(0, z - t, t, t, above).start()
+            w_relay(0, z - t, t, above, z < n - 1)
 
         @pl.when(z + t <= n - 1)
         def _():
-            w_copy(1, z + t, t, t - 1, peer).wait_recv()
-
-            @pl.when(z > 0)
-            def _():
-                w_copy(1, z + t, t, t, below).start()
+            w_relay(1, z + t, t, below, z > 0)
 
         @pl.when(z + d <= n - 1)
         def _():
@@ -247,17 +278,89 @@
 
     lax.fori_loop(1, n, slot, 0)
 
+    def core_send(c):
+        return remote(
+            delta.at[half_rows(c, 1 - core)], core_in.at[packed_rows(c)],
+            core_tx.at[c], core_rx.at[c], core_peer, "rep")
+
+    def y_send(c, k):
+        at = y_parts.at[y, packed_rows(c)]
+        return remote(at, at, y_tx.at[k, c], y_rx.at[y, c], y_peer(k), "rep")
+
+    def y_arrival(c, k):
+        source = lax.rem(y + k, pairs_y)
+        at = y_parts.at[source, packed_rows(c)]
+        return remote(at, at, y_tx.at[k, c], y_rx.at[source, c], y_peer(k), "rep")
+
+    def back_send(c, which):
+        at = delta_sum.at[half_rows(c, which)]
+        return remote(at, at, back_tx.at[c], back_rx.at[c], core_peer, "rep")
+
+    def inner_step(c):
+        span = chunk_rows(c)
+
+        @pl.when(z > 0)
+        def _():
+            z_copy(running, z + 1, 0, n - 1, n - 1, c, peer).wait_recv()
+            grad[span, :] = grad[span, :] + running[z + 1, span, :].astype(jnp.float32)
+
+        @pl.when(z < n - 1)
+        def _():
+            z_copy(running, z, 1, n - 1, n - 1, c, peer).wait_recv()
+            grad[span, :] = grad[span, :] + running[z, span, :].astype(jnp.float32)
+
+        for copy in load_state(c):
+            copy.wait()
+        at = lax.rem(c, 2)
+        g = grad[span, :]
+        weights = state[at, 0]
+        m_next = decay_one * state[at, 1] + (1.0 - decay_one) * g
+        v_next = decay_two * state[at, 2] + (1.0 - decay_two) * g * g
+        inner_next = weights - inner_rate * (m_next / (jnp.sqrt(v_next) + epsilon) + weight_decay * weights)
+        delta[span, :] = state[at, 3] - inner_next
+        core_send(c).start()
+
+        @pl.when(c + 2 < CHUNKS)
+        def _():
+            for copy in load_state(c + 2):
+                copy.start()
+
+    def over_y(c):
+        core_send(c).wait_recv()
+        y_parts[y, packed_rows(c), :] = (
+            delta[half_rows(c, core), :] + core_in[packed_rows(c), :]).astype(jnp.bfloat16)
+        for k in range(1, pairs_y):
+            y_send(c, k).start()
+
+    def back(c):
+        for k in range(1, pairs_y):
+            y_arrival(c, k).wait_recv()
+        total = y_parts[0, packed_rows(c), :].astype(jnp.float32)
+        for i in range(1, pairs_y):
+            total = total + y_parts[i, packed_rows(c), :].astype(jnp.float32)
+        delta_sum[half_rows(c, core), :] = total
+        back_send(c, core).start()
+
     partial(z)
 
-    @pl.when(z > 0)
-    def _():
-        sum_copy(0, z, n - 1, n - 1, peer).wait_recv()
-        add_in(up, z)
-
-    @pl.when(z < n - 1)
-    def _():
-        sum_copy(1, z, n - 1, n - 1, peer).wait_recv()
-        add_in(down, z)
+    @pl.loop(0, CHUNKS)
+    def _(c):
+        inner_step(c)
+        over_y(c)
+
+        @pl.when(c > 0)
+        def _():
+            back(c - 1)
+
+    back(CHUNKS - 1)
+
+    @pl.loop(0, CHUNKS)
+    def _(c):
+        back_send(c, 1 - core).wait_recv()
+        back_send(c, core).wait_send()
+        core_send(c).wait_send()
+        for k in range(1, pairs_y):
+            y_send(c, k).wait_send()
 
     @pl.loop(1, size)
     def _(k):
@@ -268,22 +371,23 @@
     @pl.loop(0, n)
     def _(j):
         send_block(j).wait_send()
-        w_way = j
-
-        @pl.when(z < n - 1)
-        def _():
-            sum_copy(0, w_way, j, j, peer).wait_send()
-
-        @pl.when(z > 0)
-        def _():
-            sum_copy(1, w_way, j, j, peer).wait_send()
+
+        @pl.loop(0, CHUNKS)
+        def _(c):
+            @pl.when(z < n - 1)
+            def _():
+                z_copy(w_all, j, 0, j, j, c, peer).wait_send()
+
+            @pl.when(z > 0)
+            def _():
+                z_copy(w_all, j, 1, j, j, c, peer).wait_send()
 
         ig_keep(j).wait()
         ig_send(j).wait_send()
         ig_arrival(j).wait_recv()
 
 
-def exchange(size, scale, acts, grads, w_half, sums, signs):
+def exchange(size, groups, scale, acts, grads, w_half, sums, signs, inner_w, adam_m, adam_v, anchor):
     n = size // 2
     rows, model = acts.shape
     feats, width = w_half.shape
@@ -292,31 +396,37 @@
     anywhere = pl.BlockSpec(memory_space=pl.ANY)
     vmem = pl.BlockSpec(memory_space=pltpu.VMEM)
     return pl.pallas_call(
-        functools.partial(exchange_kernel, size, scale),
+        functools.partial(exchange_kernel, size, groups, scale),
         out_shape=(
             jax.ShapeDtypeStruct((rows, model), bf16),
             jax.ShapeDtypeStruct((feats, width), jnp.float32),
+            jax.ShapeDtypeStruct((feats, width), jnp.float32),
         ),
-        in_specs=[anywhere, anywhere, anywhere, vmem, vmem],
-        out_specs=(anywhere, vmem),
+        in_specs=[anywhere, anywhere, anywhere, vmem, vmem] + [anywhere] * 4,
+        out_specs=(anywhere, vmem, vmem),
         scratch_shapes=[
             pltpu.VMEM((size,) + sums.shape, jnp.float32),
             pltpu.VMEM((n, 2 * rows, feats), bf16),
             pltpu.VMEM((2 * rows, width), bf16),
             pltpu.VMEM((n, feats, width), bf16),
-            pltpu.VMEM((n, feats, width), bf16),
-            pltpu.VMEM((n, feats, width), bf16),
+            pltpu.VMEM((n + 1, feats, width), bf16),
             pltpu.VMEM((n, 2 * rows, feats), bf16),
+            pltpu.VMEM((2, 4, feats // CHUNKS, width), jnp.float32),
+            pltpu.VMEM((feats, width), jnp.float32),
+            pltpu.VMEM((feats // 2, width), jnp.float32),
+            pltpu.VMEM((groups // 2, feats // 2, width), bf16),
             dma((size,)), dma((size,)), dma((2,)), dma((2,)),
             dma((n,)), dma((n,)), dma((n,)),
-            dma((2, n)), dma((2, n)),
+            dma((2, n, CHUNKS)), dma((2, n, CHUNKS)),
             dma((n,)), dma((n,)), dma((n,)),
+            dma((2, 4)), dma((CHUNKS,)), dma((CHUNKS,)),
+            dma((groups // 2, CHUNKS)), dma((groups // 2, CHUNKS)), dma((CHUNKS,)), dma((CHUNKS,)),
         ],
         compiler_params=pltpu.CompilerParams(
-            collective_id=0, has_side_effects=True, vmem_limit_bytes=60 * 1024 * 1024),
+            collective_id=0, has_side_effects=True, vmem_limit_bytes=62 * 1024 * 1024),
         cost_estimate=pl.CostEstimate(
             flops=8 * rows * model * width, bytes_accessed=6 * rows * model, transcendentals=0),
-    )(acts, grads, w_half, sums, signs)
+    )(acts, grads, w_half, sums, signs, inner_w, adam_m, adam_v, anchor)
 
 
 def outer_step(delta_avg, anchor_rows, mom_rows):
@@ -345,15 +455,11 @@
         jnp.pad(ours, ((0, 0), (0, 0), (0, tile - seqs)))[..., None], (2 * seqs, size, tile, 128))
     grads = jnp.where(loss_mask[:, None] != 0, tok_grads, jnp.zeros_like(tok_grads))
     w_half = inner_w[0].astype(jnp.bfloat16)
-    input_grad, grad = exchange(size, scale, acts, grads, w_half, sums, signs)
+    groups = lax.axis_size("rep")
+    input_grad, grad, delta_sum = exchange(
+        size, groups, scale, acts, grads, w_half, sums, signs, inner_w[0], adam_m[0], adam_v[0], anchor)
     m_next = decay_one * adam_m[0] + (1.0 - decay_one) * grad
-    v_next = decay_two * adam_v[0] + (1.0 - decay_two) * grad * grad
-    inner_next = inner_w[0] - inner_rate * (
-        m_next / (jnp.sqrt(v_next) + epsilon) + weight_decay * inner_w[0]
-    )
-    delta = anchor - inner_next
-    groups = lax.axis_size("rep")
-    delta_avg = lax.psum(delta, "rep") / groups
+    delta_avg = delta_sum / groups
     new_anchor, new_mom = outer_step(delta_avg, anchor, outer_mom)
     return (input_grad, new_anchor, new_mom, m_next[None])
 

time: 353 us -> 262 us (0.74)
  waiting for transfers between devices: 85.7 us -> 0 us
  Pallas kernels: 211 us -> 229 us
  between operations: 14.1 us -> 0.7 us
  other arithmetic: 30 us -> 21.4 us
    psum x1 -> x0, waiting for transfers between devices: 85.7 us -> none  [local(): delta_avg = lax.psum(delta, 'rep') / groups]
    pallas_call x1, Pallas kernels: 211 us -> 229 us  [exchange(): pl.pallas_call(functools.partial(exchange_kernel, size, groups, scale), o...]
    sub x1, other arithmetic: 10.6 us -> 4.95 us  [outer_step(): anchor_next = anchor_rows - outer_rate * (delta_avg + momentum * mom_next)]
    broadcast_in_dim x1, other arithmetic: 11.3 us -> 7.22 us  [local(): return (input_grad, new_anchor, new_mom, m_next[None])]
    unnamed x4 -> x8, local copies, waits for them, and re-layouts: 7.91 us -> 9.3 us
  transfers between devices with their start and end apart: 1 -> 0, of which waited for: 1 -> 0; matrix products, arithmetic and copies ran while one was open for 0% -> 0% of each run, Pallas kernels for 0% -> 0%
where the time goes in v2:
time: 262 us
  Pallas kernels  229 us (87%)
  other arithmetic  21.4 us (8%)
  local copies, waits for them, and re-layouts  10.8 us (4%)
    pallas_call x1, Pallas kernels, exchange(): pl.pallas_call(functools.partial(exchange_kernel, size, groups, scale), o...  229 us
    unnamed x8, local copies, waits for them, and re-layouts  9.3 us
    broadcast_in_dim x1, other arithmetic, local(): return (input_grad, new_anchor, new_mom, m_next[None])  7.22 us

profile of v2, /device:TPU:13, one launch (start us, length us, event | category | flops | bytes accessed | tf_op | source)
XLA Modules:
  0.0 261.7 jit_solution(2070949928441085626)
XLA Ops:
  0.6 0.7 broadcast_compare_fusion
  1.3 0.7 broadcast_add_fusion
  2.0 0.7 convert_multiply_fusion
  2.7 0.1 reduce_sum.18
  2.8 0.1 convert_subtract_fusion
  2.9 0.7 scatter.8.sums
  3.6 0.7 fusion
  4.3 0.1 multiply_reduce_fusion
  4.4 0.1 copy.18
  4.5 0.1 copy.20
  4.6 0.8 broadcast_in_dim.13.signs
  5.4 2.3 broadcast_select_fusion.grads
  7.7 3.8 %bitcast_convert_fusion.w_own = bf16[1024,1024]{1,0:T(8,128)(2,1)} fusion(f32[1,1024,1024]{2,1,0:T(8,128)} %param.17), kind=kLoop, calls=%fused_computation.20 | loop fusion | flops 1048576 | bytes 6291456 | tf_op jit(solution)/shard_map/convert_element_type | solution.py:457
  11.6 228.7 %shard_map.129 = (bf16[512,8192]{1,0:T(8,128)(2,1)}, f32[1024,1024]{1,0:T(8,128)}, f32[1024,1024]{1,0:T(8,128)}) custom-call(bf16[512,8192]{1,0:T(8,128)(2,1)} %acts.1, bf16[512,1024]{1,0:T(8,128)(2,1)} %broadcast_select_fusion.grads, bf16[1024,1024]{1,0:T(8,128)(2,1)} %bitcast_convert_fusion.w_own, f32[8,128]{1,0:T(8,128)} %scatter.8.sums, ...), custom_call_target="tpu_custom_call" | custom-call | flops 34359738368 | bytes 25165824 | tf_op jit(solution)/shard_map/pallas_call | solution.py:398
  240.3 0.0 copy-start
  240.3 0.0 copy-start.1
  240.3 0.0 copy-start.2
  240.3 7.2 %add_bitcast_fusion = f32[1,1024,1024]{2,1,0:T(8,128)} fusion(f32[1024,1024]{1,0:T(8,128)} %get-tuple-element.21, f32[1,1024,1024]{2,1,0:T(8,128)} %param.18), kind=kLoop, calls=%fused_computation | loop fusion | flops 3145728 | bytes 12582912 | tf_op jit(solution)/shard_map/broadcast_in_dim | solution.py:464
  247.6 0.0 copy-done
  247.6 0.0 copy-done.1
  247.6 1.4 copy-done.2
  248.9 5.0 %multiply_subtract_fusion = (f32[1024,1024]{1,0:T(8,128)}, f32[1024,1024]{1,0:T(8,128)}) fusion(f32[1024,1024]{1,0:T(8,128)S(1)} %copy-done, f32[1024,1024]{1,0:T(8,128)S(1)} %copy-done.2, f32[1024,1024]{1,0:T(8,128)S(1)} %copy-done.1), kind=kLoop, calls=%fused_computation.1 | loop fusion | flops 7340032 | bytes 20971520 | tf_op jit(solution)/shard_map/sub | solution.py:434
  253.9 7.8 %copy.22 = bf16[512,8192]{1,0:T(8,128)(2,1)} copy(bf16[512,8192]{1,0:T(8,128)(2,1)} %get-tuple-element.30) | data formatting | bytes 16777216
  (5 shorter events, 0.1 us)
Async XLA Ops:
  240.3 7.3 %copy-start = (f32[1024,1024]{1,0:T(8,128)S(1)}, f32[1024,1024]{1,0:T(8,128)}, u32[]{:S(2)}) copy-start(f32[1024,1024]{1,0:T(8,128)} %anchor.1) | copy-start | bytes 12582916
  240.3 7.3 %copy-start.1 = (f32[1024,1024]{1,0:T(8,128)S(1)}, f32[1024,1024]{1,0:T(8,128)}, u32[]{:S(2)}) copy-start(f32[1024,1024]{1,0:T(8,128)} %param.21) | copy-start | bytes 12582916
  240.3 8.6 %copy-start.2 = (f32[1024,1024]{1,0:T(8,128)S(1)}, f32[1024,1024]{1,0:T(8,128)}, u32[]{:S(2)}) copy-start(f32[1024,1024]{1,0:T(8,128)} %get-tuple-element.20) | copy-start | bytes 12582916

commit v3 on v2

--- a/solution.py
+++ b/solution.py
@@ -33,7 +33,7 @@
 
 
 def exchange_kernel(
-    size, groups, scale, acts, grads, w_own, sums, signs, inner_w, adam_m, adam_v, anchor,
+    size, groups, scale, acts, grads, sums, signs, inner_w, adam_m, adam_v, anchor,
     input_grad, grad, delta_sum,
     all_sums, act, cot, w_all, running, stage, state, delta, core_in, y_parts,
     sums_tx, sums_rx, g_sem, local_sem, act_local, act_tx, act_rx, z_tx, z_rx, ig_local, ig_tx, ig_rx,
@@ -45,7 +45,7 @@
     peer = z * 2 + (1 - x)
     above, below = lax.rem(me + 2, size), lax.rem(me + size - 2, size)
     rows = acts.shape[0]
-    feats, width = w_own.shape
+    feats, width = inner_w.shape
     part = min(256, feats)
     parts = feats // part
     seqs = rows // SEQLEN
@@ -103,14 +103,16 @@
         def _(c):
             z_copy(w_all, j, way, t, t, c, target).start()
 
-    def w_relay(way, j, t, target, further):
+    def w_relay(way, j, t, target):
         @pl.loop(0, CHUNKS)
         def _(c):
             z_copy(w_all, j, way, t, t - 1, c, peer).wait_recv()
-
-            @pl.when(further)
-            def _():
-                z_copy(w_all, j, way, t, t, c, target).start()
+            z_copy(w_all, j, way, t, t, c, target).start()
+
+    def w_arrive(way, j, t):
+        @pl.loop(0, CHUNKS)
+        def _(c):
+            z_copy(w_all, j, way, t, t - 1, c, peer).wait_recv()
 
     def load_state(c):
         at = lax.rem(c, 2)
@@ -119,7 +121,7 @@
             for i, array in enumerate((inner_w, adam_m, adam_v, anchor))
         ]
 
-    own_w = pltpu.make_async_copy(w_own, w_all.at[z], local_sem.at[0])
+    own_w = pltpu.make_async_copy(inner_w, grad, local_sem.at[0])
     own_g = pltpu.make_async_copy(grads, cot.at[pl.ds(0, rows)], local_sem.at[1])
     own_w.start()
     own_g.start()
@@ -143,6 +145,13 @@
     pl.semaphore_signal(barrier, inc=1, device_id={"rep": core_peer}, device_id_type=MESH)
     for k in range(1, pairs_y):
         pl.semaphore_signal(barrier, inc=1, device_id={"rep": y_peer(k)}, device_id_type=MESH)
+
+    own_w.wait()
+
+    @pl.loop(0, CHUNKS)
+    def _(c):
+        w_all[z, chunk_rows(c), :] = grad[chunk_rows(c), :].astype(jnp.bfloat16)
+
     pl.semaphore_wait(barrier, size - 1 + pairs_y)
 
     @pl.loop(1, size)
@@ -151,7 +160,6 @@
 
     peer_g = remote(grads, cot.at[pl.ds(rows, rows)], g_sem.at[0], g_sem.at[1], peer)
     peer_g.start()
-    own_w.wait()
 
     @pl.when(z < n - 1)
     def _():
@@ -161,7 +169,8 @@
     def _():
         w_send(1, z, 0, below)
 
-    send_acts(n - 1)
+    farthest = jnp.maximum(z, n - 1 - z)
+    send_acts(farthest)
 
     @pl.loop(1, size)
     def _(k):
@@ -170,8 +179,7 @@
 
     own_g.wait()
     peer_g.wait_recv()
-    if n >= 2:
-        send_acts(n - 2)
+    send_acts(farthest - 1)
     half_n = size * seqs // 2
     for q in range(2 * seqs):
         owner = me if q < seqs else peer
@@ -198,7 +206,6 @@
         at = j + 1 if way == 0 else j
         has_source = z > 0 if way == 0 else z < n - 1
         target = above if way == 0 else below
-        partial(j)
 
         @pl.loop(0, CHUNKS)
         def _(c):
@@ -242,36 +249,60 @@
     def slot(t, carry):
         d = n - t
 
+        sum_up = z + d <= n - 1
+        sum_down = z - d >= 0
+        both = jnp.logical_and(sum_up, sum_down)
+
+        @pl.when(sum_up)
+        def _():
+            partial(z + d)
+
+        @pl.when(jnp.logical_and(sum_down, jnp.logical_not(sum_up)))
+        def _():
+            partial(z - d)
+
+        @pl.when(jnp.logical_and(z >= t, z < n - 1))
+        def _():
+            w_relay(0, z - t, t, above)
+
+        @pl.when(jnp.logical_and(z + t <= n - 1, z > 0))
+        def _():
+            w_relay(1, z + t, t, below)
+
+        @pl.when(sum_up)
+        def _():
+            pass_on(0, z + d, t)
+
+        @pl.when(both)
+        def _():
+            partial(z - d)
+
+        @pl.when(sum_down)
+        def _():
+            pass_on(1, z - d, t)
+
+        @pl.when(farthest - 1 - t >= 0)
+        def _():
+            send_acts(farthest - 1 - t)
+
+        @pl.when(t == 1)
+        def _():
+            ig_block(z)
+
         @pl.when(z >= t)
         def _():
-            w_relay(0, z - t, t, above, z < n - 1)
+            @pl.when(z == n - 1)
+            def _():
+                w_arrive(0, z - t, t)
+
+            ig_block(z - t)
 
         @pl.when(z + t <= n - 1)
         def _():
-            w_relay(1, z + t, t, below, z > 0)
-
-        @pl.when(z + d <= n - 1)
-        def _():
-            pass_on(0, z + d, t)
-
-        @pl.when(z - d >= 0)
-        def _():
-            pass_on(1, z - d, t)
-
-        @pl.when(d >= 2)
-        def _():
-            send_acts(d - 2)
-
-        @pl.when(t == 1)
-        def _():
-            ig_block(z)
-
-        @pl.when(z >= t)
-        def _():
-            ig_block(z - t)
-
-        @pl.when(z + t <= n - 1)
-        def _():
+            @pl.when(z == 0)
+            def _():
+                w_arrive(1, z + t, t)
+
             ig_block(z + t)
 
         return carry
@@ -387,10 +418,10 @@
         ig_arrival(j).wait_recv()
 
 
-def exchange(size, groups, scale, acts, grads, w_half, sums, signs, inner_w, adam_m, adam_v, anchor):
+def exchange(size, groups, scale, acts, grads, sums, signs, inner_w, adam_m, adam_v, anchor):
     n = size // 2
     rows, model = acts.shape
-    feats, width = w_half.shape
+    feats, width = inner_w.shape
     dma = pltpu.SemaphoreType.DMA
     bf16 = jnp.bfloat16
     anywhere = pl.BlockSpec(memory_space=pl.ANY)
@@ -402,7 +433,7 @@
             jax.ShapeDtypeStruct((feats, width), jnp.float32),
             jax.ShapeDtypeStruct((feats, width), jnp.float32),
         ),
-        in_specs=[anywhere, anywhere, anywhere, vmem, vmem] + [anywhere] * 4,
+        in_specs=[anywhere, anywhere, vmem, vmem] + [anywhere] * 4,
         out_specs=(anywhere, vmem, vmem),
         scratch_shapes=[
             pltpu.VMEM((size,) + sums.shape, jnp.float32),
@@ -426,7 +457,7 @@
             collective_id=0, has_side_effects=True, vmem_limit_bytes=62 * 1024 * 1024),
         cost_estimate=pl.CostEstimate(
             flops=8 * rows * model * width, bytes_accessed=6 * rows * model, transcendentals=0),
-    )(acts, grads, w_half, sums, signs, inner_w, adam_m, adam_v, anchor)
+    )(acts, grads, sums, signs, inner_w, adam_m, adam_v, anchor)
 
 
 def outer_step(delta_avg, anchor_rows, mom_rows):
@@ -454,10 +485,9 @@
     signs = jnp.broadcast_to(
         jnp.pad(ours, ((0, 0), (0, 0), (0, tile - seqs)))[..., None], (2 * seqs, size, tile, 128))
     grads = jnp.where(loss_mask[:, None] != 0, tok_grads, jnp.zeros_like(tok_grads))
-    w_half = inner_w[0].astype(jnp.bfloat16)
     groups = lax.axis_size("rep")
     input_grad, grad, delta_sum = exchange(
-        size, groups, scale, acts, grads, w_half, sums, signs, inner_w[0], adam_m[0], adam_v[0], anchor)
+        size, groups, scale, acts, grads, sums, signs, inner_w[0], adam_m[0], adam_v[0], anchor)
     m_next = decay_one * adam_m[0] + (1.0 - decay_one) * grad
     delta_avg = delta_sum / groups
     new_anchor, new_mom = outer_step(delta_avg, anchor, outer_mom)

time: 262 us -> 247 us (0.943)
  Pallas kernels: 229 us -> 216 us
  other arithmetic: 21.4 us -> 17.6 us
    pallas_call x1, Pallas kernels: 229 us -> 216 us  [exchange(): pl.pallas_call(functools.partial(exchange_kernel, size, groups, scale), o...]
    convert_element_type x1 -> x0, other arithmetic: 3.83 us -> none  [local(): w_half = inner_w[0].astype(jnp.bfloat16)]
where the time goes in v3:
time: 247 us; the launch traced here: 245 us
  Pallas kernels  216 us (87%)
  other arithmetic  17.6 us (7%)
  local copies, waits for them, and re-layouts  10.8 us (4%)
    pallas_call x1, Pallas kernels, exchange(): pl.pallas_call(functools.partial(exchange_kernel, size, groups, scale), o...  216 us
    unnamed x8, local copies, waits for them, and re-layouts  9.3 us
    broadcast_in_dim x1, other arithmetic, local(): return (input_grad, new_anchor, new_mom, m_next[None])  7.22 us
    sub x1, other arithmetic, outer_step(): anchor_next = anchor_rows - outer_rate * (delta_avg + momentum * mom_next)  4.95 us

profile of v3, /device:TPU:13, one launch (start us, length us, event | category | flops | bytes accessed | tf_op | source)
XLA Modules:
  0.0 245.0 jit_solution(15441843177667839427)
XLA Ops:
  0.6 0.7 broadcast_compare_fusion
  1.3 0.7 broadcast_add_fusion
  2.0 0.7 convert_multiply_fusion
  2.7 0.1 reduce_sum.18
  2.8 0.1 convert_subtract_fusion
  2.9 0.7 scatter.8.sums
  3.6 0.7 fusion
  4.3 0.1 multiply_reduce_fusion
  4.4 0.1 copy.18
  4.5 0.1 copy.20
  4.6 0.8 broadcast_in_dim.13.signs
  5.4 2.3 broadcast_select_fusion.grads
  7.7 215.9 %shard_map.129 = (bf16[512,8192]{1,0:T(8,128)(2,1)}, f32[1024,1024]{1,0:T(8,128)}, f32[1024,1024]{1,0:T(8,128)}) custom-call(bf16[512,8192]{1,0:T(8,128)(2,1)} %acts.1, bf16[512,1024]{1,0:T(8,128)(2,1)} %broadcast_select_fusion.grads, f32[8,128]{1,0:T(8,128)} %scatter.8.sums, f32[4,8,8,128]{3,2,1,0:T(8,128)} %broadcast_in_dim.13.signs, ...), custom_call_target="tpu_custom_call" | custom-call | flops 34359738368 | bytes 25165824 | tf_op jit(solution)/shard_map/pallas_call | solution.py:429
  223.7 0.0 copy-start
  223.7 0.0 copy-start.1
  223.7 0.0 copy-start.2
  223.7 7.2 %add_bitcast_fusion = f32[1,1024,1024]{2,1,0:T(8,128)} fusion(f32[1024,1024]{1,0:T(8,128)} %get-tuple-element.21, f32[1,1024,1024]{2,1,0:T(8,128)} %param.18), kind=kLoop, calls=%fused_computation | loop fusion | flops 3145728 | bytes 12582912 | tf_op jit(solution)/shard_map/broadcast_in_dim | solution.py:494
  230.9 0.0 copy-done
  230.9 0.0 copy-done.1
  230.9 1.4 copy-done.2
  232.3 5.0 %multiply_subtract_fusion = (f32[1024,1024]{1,0:T(8,128)}, f32[1024,1024]{1,0:T(8,128)}) fusion(f32[1024,1024]{1,0:T(8,128)S(1)} %copy-done, f32[1024,1024]{1,0:T(8,128)S(1)} %copy-done.2, f32[1024,1024]{1,0:T(8,128)S(1)} %copy-done.1), kind=kLoop, calls=%fused_computation.1 | loop fusion | flops 7340032 | bytes 20971520 | tf_op jit(solution)/shard_map/sub | solution.py:465
  237.3 7.8 %copy.22 = bf16[512,8192]{1,0:T(8,128)(2,1)} copy(bf16[512,8192]{1,0:T(8,128)(2,1)} %get-tuple-element.30) | data formatting | bytes 16777216
  (5 shorter events, 0.1 us)
Async XLA Ops:
  223.7 7.3 %copy-start = (f32[1024,1024]{1,0:T(8,128)S(1)}, f32[1024,1024]{1,0:T(8,128)}, u32[]{:S(2)}) copy-start(f32[1024,1024]{1,0:T(8,128)} %anchor.1) | copy-start | bytes 12582916
  223.7 7.3 %copy-start.1 = (f32[1024,1024]{1,0:T(8,128)S(1)}, f32[1024,1024]{1,0:T(8,128)}, u32[]{:S(2)}) copy-start(f32[1024,1024]{1,0:T(8,128)} %param.21) | copy-start | bytes 12582916
  223.7 8.6 %copy-start.2 = (f32[1024,1024]{1,0:T(8,128)S(1)}, f32[1024,1024]{1,0:T(8,128)}, u32[]{:S(2)}) copy-start(f32[1024,1024]{1,0:T(8,128)} %get-tuple-element.20) | copy-start | bytes 12582916
